TPU v7x, 32 devices: a whole 2x2x4 slice. The times are simulated.
32 devices in a mesh: groups: 2 (over y), row: 4 (over z), col: 4 (over x, core).
Axes of the slice: x: 2, y: 2, z: 4, core: 2. Of those that a mesh axis runs over, the one named last changes fastest.
Arguments:
- src_points: bfloat16 [256, 128, 64], P(('groups', 'row')), parts along dimension 0, may hold values from -8 to 8, as said below
- tgt_points: bfloat16 [1024, 128, 64], P(('groups', 'col')), parts along dimension 0, may hold values from -8 to 8, as said below
- src_logw: float32 [256, 128], P(('groups', 'row')), parts along dimension 0, may hold values from -1 to 1
- tgt_logw: float32 [1024, 128], P(('groups', 'col')), parts along dimension 0, may hold values from -1 to 1
- src_sizes: int32 [256], P(('groups', 'row')), parts along dimension 0, may hold values from 64 to 128, as said below
- tgt_sizes: int32 [1024], P(('groups', 'col')), parts along dimension 0, may hold values from 64 to 128, as said below
- pattern: int32 [256, 4, 8], P(('groups', 'row'), 'col'), parts along dimension 0, may hold values from 0 to 127, as said below
- counts: int32 [256, 4], P(('groups', 'row'), 'col'), parts along dimension 0, may hold values from 1 to 8, as said below
Outputs:
- field_f: float32 [256, 128], P(('groups', 'row')), parts along dimension 0
- field_g: float32 [1024, 128], P(('groups', 'col')), parts along dimension 0
There are 2 independent parts, one for each index of `groups`. A program takes and returns all parts, laid end to end along the dimension named above; each array names one. Nothing has to cross between parts.
Inputs may be any that keep to these rules, and one draw needn't show every extreme that they name: `src_sizes`: real cells fill a block from slot 0; some block has exactly 128 and some exactly 64. `tgt_sizes`: real cells fill a block from slot 0; some block has exactly 128 and some exactly 64. The 8 entries of pattern[s, c] are distinct; in every column shard exactly two target blocks, never the first or the last of the shard, appear in no entry of pattern, so they have no neighbours. `counts`: every source block has at least one neighbour in every column shard; some pair (s, c) has 8. `src_points`: coordinates are cluster centres plus noise. `tgt_points`: coordinates are cluster centres plus noise.
All inputs are finite; a program needn't handle non-finite values.
Results may differ from a plain program's by a relative error of at most 0.0003.
Values sent between devices are 32-bit elements; how exact they have to be, the bound alone decides.
No kernel may reach another device: no remote copies, remote signals or barrier semaphores. Data moves between devices by JAX's collectives and lax.ppermute only.
A program may use at most 64 MiB of HBM per device.

v0:
```python
import functools
import math

import jax
import jax.numpy as jnp
from jax import lax
from jax.experimental import pallas as pl
from jax.experimental.pallas import tpu as pltpu
from jax.sharding import PartitionSpec as P

ITERS = 2
EPS = 0.5
LOG2E = math.log2(math.e)
SCALE = 2.0 / EPS * LOG2E
FIELD = EPS / LOG2E
FLOOR = -1e30
ABSENT = -1e29
SMALL = 2.0**-80
CHUNK = 16
EXTRA = 16
VMEM_LIMIT = 26 * 1024 * 1024


def eight(t):
    return pl.ds(pl.multiple_of(t * 8, 8), 8)


def folded(matrix):
    return matrix.reshape(-1, 8, matrix.shape[-1])


def every_eighth(ref, r, count):
    return ref[pl.ds(r, count, stride=8), :]


def merged(parts):
    top = functools.reduce(jnp.maximum, parts)
    total = top + jnp.log2(sum(jnp.exp2(part - top) for part in parts))
    return top > ABSENT, total


def spread(p_ref, pb_ref):
    blocks, size = p_ref.shape

    def body(s, carry):
        pb_ref[s] = jnp.broadcast_to(p_ref[pl.ds(s, 1), :], (size, size)).T
        return carry

    lax.fori_loop(0, blocks, body, 0, unroll=16)


def collect(acc_ref, sum_ref):
    def body(s, carry):
        sum_ref[pl.ds(s, 1), :] = jnp.sum(acc_ref[s].T, axis=0, keepdims=True)
        return carry

    lax.fori_loop(0, acc_ref.shape[0], body, 0, unroll=16)


def row_result(total, shift, valid, z_ref, q_ref, lists, pairs, out_ref):
    blocks, size = out_ref.shape
    out_ref[...] = jnp.where(valid, jnp.log2(jnp.maximum(total, SMALL)) - shift, FLOOR)
    lowest = jnp.min(jnp.where(valid, total, 1.0))

    @pl.when(lowest < SMALL)
    def _():
        def score(p):
            z = z_ref[p]
            return z if q_ref is None else z + q_ref[pl.ds(lists[lists.shape[0] // 2 + p], 1), :]

        def block(s, first):
            def same(p):
                return (p < pairs) & (lists[jnp.minimum(p, pairs - 1)] == s)

            def raise_top(carry):
                return carry[0] + 1, jnp.maximum(carry[1], score(carry[0]))

            start = (first, jnp.full((size, size), 2.0 * FLOOR, jnp.float32))
            end, top = lax.while_loop(lambda carry: same(carry[0]), raise_top, start)
            top = jnp.max(top, axis=1, keepdims=True)

            def add(p, acc):
                return acc + jnp.exp2(score(p) - top)

            acc = lax.fori_loop(first, end, add, jnp.zeros((size, size), jnp.float32))
            full = top + jnp.log2(jnp.sum(acc, axis=1, keepdims=True))
            out_ref[pl.ds(s, 1), :] = jnp.broadcast_to(full, (size, size)).T[:1, :]
            return end

        lax.fori_loop(0, blocks, block, 0)
        out_ref[...] = jnp.where(valid, out_ref[...], FLOOR)


def col_pass(z_ref, pb_ref, q_ref, touched_ref, lists, pairs, acc_ref, top_ref, out_ref):
    targets = out_ref.shape[0]
    room = lists.shape[0] // 2
    acc_ref[...] = jnp.zeros_like(acc_ref)

    def chunk(c, carry):
        for k in range(CHUNK):
            s, t = lists[c * CHUNK + k], lists[room + c * CHUNK + k]
            z = z_ref[c * CHUNK + k] + pb_ref[s]
            if q_ref is not None:
                z = z + q_ref[pl.ds(t, 1), :]
            acc_ref[eight(t), :] += jnp.sum(folded(jnp.exp2(z)), axis=0)
        return carry

    lax.fori_loop(0, (pairs + CHUNK - 1) // CHUNK, chunk, 0)
    total = sum(every_eighth(acc_ref, r, targets) for r in range(8))
    valid = touched_ref[:targets, :] > 0.0
    shift = 0.0 if q_ref is None else q_ref[:targets, :]
    out_ref[...] = jnp.where(valid, jnp.log2(jnp.maximum(total, SMALL)) - shift, FLOOR)
    lowest = jnp.min(jnp.where(valid, total, 1.0))

    @pl.when(lowest < SMALL)
    def _():
        acc_ref[...] = jnp.zeros_like(acc_ref)
        top_ref[...] = jnp.full_like(top_ref, 2.0 * FLOOR)

        def raise_top(p, carry):
            s, t = lists[p], lists[room + p]
            z = z_ref[p] + pb_ref[s]
            top_ref[eight(t), :] = jnp.maximum(top_ref[eight(t), :], jnp.max(folded(z), axis=0))
            return carry

        lax.fori_loop(0, pairs, raise_top, 0)
        top = functools.reduce(jnp.maximum, [every_eighth(top_ref, r, targets) for r in range(8)])
        out_ref[...] = top

        def add(p, carry):
            s, t = lists[p], lists[room + p]
            z = z_ref[p] + pb_ref[s] - out_ref[pl.ds(t, 1), :]
            acc_ref[eight(t), :] += jnp.sum(folded(jnp.exp2(z)), axis=0)
            return carry

        lax.fori_loop(0, pairs, add, 0)
        exact = sum(every_eighth(acc_ref, r, targets) for r in range(8))
        out_ref[...] = jnp.where(valid, top + jnp.log2(jnp.maximum(exact, 1.0)), FLOOR)


def three_terms(row):
    high = row.astype(jnp.bfloat16)
    rest = row - high.astype(jnp.float32)
    middle = rest.astype(jnp.bfloat16)
    low = (rest - middle.astype(jnp.float32)).astype(jnp.bfloat16)
    return [high.astype(jnp.float32), middle.astype(jnp.float32), low.astype(jnp.float32)]


def extra_rows(row, first, width):
    place = lax.broadcasted_iota(jnp.int32, (EXTRA, width), 0)
    result = jnp.where((place < 6) & ((place < first) | (place >= first + 3)), 1.0, 0.0)
    for k, term in enumerate(three_terms(row)):
        result = jnp.where(place == first + k, term, result)
    return result.astype(jnp.bfloat16)


def first_kernel(
    ssz_any, tsz_any, pat_any, cnt_any, xt_any, yt_any,
    z_ref, touched_ref, lists_ref, out_ref,
    ssz_ref, tsz_ref, pat_ref, cnt_ref, lists_smem, xt_ref, x_ref, y_ref, mask_ref, live_ref, acc_ref, sum_ref, sems,
):
    blocks, size = out_ref.shape
    dims = xt_ref.shape[1]
    targets = yt_any.shape[0]
    slots = pat_ref.shape[0]
    room = lists_smem.shape[0] // 2
    small = [
        pltpu.make_async_copy(source, target, sems.at[k])
        for k, (source, target) in enumerate(
            [(ssz_any, ssz_ref), (tsz_any, tsz_ref), (pat_any, pat_ref), (cnt_any, cnt_ref)]
        )
    ]
    copy_x = pltpu.make_async_copy(xt_any, xt_ref, sems.at[4])
    copy_y = pltpu.make_async_copy(yt_any, y_ref.at[pl.ds(0, targets), pl.ds(0, dims), :], sems.at[5])
    for copy in small:
        copy.start()
    copy_x.start()
    copy_y.start()
    acc_ref[...] = jnp.zeros_like(acc_ref)
    touched_ref[...] = jnp.zeros_like(touched_ref)
    y_ref[targets] = jnp.zeros(y_ref.shape[1:], jnp.bfloat16)
    mask_ref[pl.ds(targets, 8), :] = jnp.zeros((8, size), jnp.float32)
    lanes = lax.broadcasted_iota(jnp.int32, (1, size), 1)
    y_ref[targets, pl.ds(dims, EXTRA), :] = extra_rows(jnp.full((1, size), FLOOR, jnp.float32), 3, size)
    for copy in small:
        copy.wait()

    def list_block(s, p):
        count = cnt_ref[s]
        for k in range(slots):
            lists_smem[p] = s
            lists_smem[room + p] = pat_ref[k, s]
            p = p + (k < count).astype(jnp.int32)
        return p

    pairs = lax.fori_loop(0, blocks, list_block, 0)
    for k in range(CHUNK):
        lists_smem[pairs + k] = blocks - 1
        lists_smem[room + pairs + k] = targets
    lists_smem[room - 1] = pairs
    copy_lists = pltpu.make_async_copy(lists_smem, lists_ref, sems.at[6])
    copy_lists.start()
    copy_x.wait()

    def source(s, carry):
        xt = xt_ref[s].astype(jnp.float32)
        live = lanes < ssz_ref[s]
        norm = jnp.where(live, -0.5 * jnp.sum(xt * xt, axis=0, keepdims=True), FLOOR)
        live_ref[pl.ds(s, 1), :] = live.astype(jnp.float32)
        extra = extra_rows(norm, 0, size).astype(jnp.float32)
        x_ref[s] = jnp.concatenate([xt, extra], axis=0).T.astype(jnp.bfloat16)
        return carry

    lax.fori_loop(0, blocks, source, 0, unroll=4)
    copy_y.wait()

    def target(t, carry):
        yt = y_ref[t, pl.ds(0, dims), :].astype(jnp.float32)
        live = lanes < tsz_ref[t]
        norm = jnp.where(live, -0.5 * jnp.sum(yt * yt, axis=0, keepdims=True), FLOOR)
        mask_ref[pl.ds(t, 1), :] = live.astype(jnp.float32)
        y_ref[t, pl.ds(dims, EXTRA), :] = extra_rows(norm, 3, size)
        return carry

    lax.fori_loop(0, targets, target, 0, unroll=8)

    def chunk(c, carry):
        for k in range(CHUNK):
            s, t = lists_smem[c * CHUNK + k], lists_smem[room + c * CHUNK + k]
            z = jnp.dot(x_ref[s], y_ref[t], preferred_element_type=jnp.float32) * SCALE
            z_ref[c * CHUNK + k] = z
            acc_ref[s] += jnp.exp2(z)
            touched_ref[pl.ds(t, 1), :] = mask_ref[pl.ds(t, 1), :]
        return carry

    lax.fori_loop(0, (pairs + CHUNK - 1) // CHUNK, chunk, 0)
    collect(acc_ref, sum_ref)
    valid = live_ref[...] > 0.0
    row_result(sum_ref[...], 0.0, valid, z_ref, None, lists_smem, pairs, out_ref)
    copy_lists.wait()


def col_kernel(n_parts, has_q, last, lists_ref, z_ref, touched_ref, logw_ref, *rest):
    q_ref, rest = (rest[0], rest[1:]) if has_q else (None, rest)
    parts, rest = rest[:n_parts], rest[n_parts:]
    p_ref, out_ref, pb_ref, lists_smem, acc_ref, top_ref, sem = rest
    copy = pltpu.make_async_copy(lists_ref, lists_smem, sem)
    copy.start()
    valid, total = merged([part[...] for part in parts])
    p_ref[...] = jnp.where(valid, LOG2E * logw_ref[...] - total, 0.0)
    spread(p_ref, pb_ref)
    copy.wait()
    room = lists_smem.shape[0] // 2
    col_pass(
        z_ref, pb_ref, q_ref, touched_ref, lists_smem, lists_smem[room - 1], acc_ref, top_ref, out_ref
    )
    if last:
        p_ref[...] = p_ref[...] * FIELD


def row_kernel(n_parts, lists_ref, z_ref, p_ref, pb_ref, earlier_ref, logw_ref, *rest):
    parts, (q_ref, out_ref, lists_smem, acc_ref, sum_ref, sem) = rest[:n_parts], rest[n_parts:]
    targets = logw_ref.shape[0]
    copy = pltpu.make_async_copy(lists_ref, lists_smem, sem)
    copy.start()
    valid, total = merged([part[...] for part in parts])
    q_ref[pl.ds(0, targets), :] = jnp.where(valid, LOG2E * logw_ref[...] - total, 0.0)
    q_ref[pl.ds(targets, 8), :] = jnp.zeros((8, q_ref.shape[1]), jnp.float32)
    acc_ref[...] = jnp.zeros_like(acc_ref)
    copy.wait()
    room = lists_smem.shape[0] // 2
    pairs = lists_smem[room - 1]

    def chunk(c, carry):
        for k in range(CHUNK):
            s, t = lists_smem[c * CHUNK + k], lists_smem[room + c * CHUNK + k]
            acc_ref[s] += jnp.exp2(z_ref[c * CHUNK + k] + pb_ref[s] + q_ref[pl.ds(t, 1), :])
        return carry

    lax.fori_loop(0, (pairs + CHUNK - 1) // CHUNK, chunk, 0)
    collect(acc_ref, sum_ref)
    row_result(
        sum_ref[...], p_ref[...], earlier_ref[...] > ABSENT, z_ref, q_ref,
        lists_smem, pairs, out_ref,
    )


def last_kernel(n_parts, logw_ref, *rest):
    parts, (out_ref,) = rest[:n_parts], rest[n_parts:]
    valid, total = merged([part[...] for part in parts])
    out_ref[...] = jnp.where(valid, (LOG2E * logw_ref[...] - total) * FIELD, 0.0)


def call(kernel, name, outs, scratch, args, spaces="v"):
    where = {"v": pltpu.VMEM, "h": pltpu.HBM}
    return pl.pallas_call(
        kernel,
        out_shape=outs,
        in_specs=[pl.BlockSpec(memory_space=where[k]) for k in (spaces * len(args))[: len(args)]],
        out_specs=[pl.BlockSpec(memory_space=pltpu.VMEM)] * len(outs),
        scratch_shapes=scratch,
        name=name,
        compiler_params=pltpu.CompilerParams(vmem_limit_bytes=VMEM_LIMIT),
    )(*args)


def exchanged(part, axis):
    size = lax.axis_size(axis)
    pieces = [part]
    for d in range(1, size):
        if size & (size - 1):
            pairs = [(i, (i + d) % size) for i in range(size)]
        else:
            pairs = [(i, i ^ d) for i in range(size)]
        pieces.append(lax.ppermute(part, axis, pairs))
    return pieces


def on_device(src_points, tgt_points, src_logw, tgt_logw, src_sizes, tgt_sizes, pattern, counts):
    blocks, size, dims = src_points.shape
    targets = tgt_points.shape[0]
    slots = pattern.shape[2]
    f32, i32, bf16 = jnp.float32, jnp.int32, jnp.bfloat16
    xt = jnp.swapaxes(src_points, 1, 2)
    yt = jnp.swapaxes(tgt_points, 1, 2)
    room = -(-(blocks * slots + CHUNK + 1) // 512) * 512
    struct = jax.ShapeDtypeStruct
    dma = pltpu.SemaphoreType.DMA
    wide = pltpu.VMEM((blocks, size, size), f32)
    sums = pltpu.VMEM((blocks, size), f32)
    acc_col = pltpu.VMEM(((targets + 8) * 8, size), f32)
    lists_smem = pltpu.SMEM((2 * room,), i32)

    z, touched, lists, row_part = call(
        first_kernel,
        "scores_and_rows",
        [
            struct((blocks * slots + CHUNK, size, size), f32),
            struct((targets + 8, size), f32),
            struct((2 * room,), i32),
            struct((blocks, size), f32),
        ],
        [
            pltpu.SMEM((blocks,), i32),
            pltpu.SMEM((targets,), i32),
            pltpu.SMEM((slots, blocks), i32),
            pltpu.SMEM((blocks,), i32),
            lists_smem,
            pltpu.VMEM((blocks, dims, size), bf16),
            pltpu.VMEM((blocks, size, dims + EXTRA), bf16),
            pltpu.VMEM((targets + 1, dims + EXTRA, size), bf16),
            pltpu.VMEM((targets + 8, size), f32),
            sums,
            wide,
            sums,
            dma((7,)),
        ],
        [src_sizes, tgt_sizes, pattern[:, 0, :].T, counts[:, 0], xt, yt],
        "h",
    )
    first_part = row_part
    q = None
    for repeat in range(ITERS):
        last = repeat == ITERS - 1
        row_parts = exchanged(row_part, "col")
        results = call(
            functools.partial(col_kernel, len(row_parts), q is not None, last),
            "columns",
            [struct((blocks, size), f32), struct((targets, size), f32)]
            + ([] if last else [struct((blocks, size, size), f32)]),
            ([wide] if last else []) + [lists_smem, acc_col, acc_col, dma],
            [lists, z, touched, src_logw] + ([] if q is None else [q]) + row_parts,
        )
        p, col_part, *pb = results
        col_parts = exchanged(col_part, "row")
        if not last:
            q, row_part = call(
                functools.partial(row_kernel, len(col_parts)),
                "rows",
                [struct((targets + 8, size), f32), struct((blocks, size), f32)],
                [lists_smem, wide, sums, dma],
                [lists, z, p, *pb, first_part, tgt_logw] + col_parts,
            )
    (field_g,) = call(
        functools.partial(last_kernel, len(col_parts)),
        "target_field",
        [struct((targets, size), f32)],
        [],
        [tgt_logw] + col_parts,
    )
    return p, field_g


def solution(mesh):
    return jax.shard_map(
        on_device,
        mesh=mesh,
        in_specs=(
            P(("groups", "row"), None, None),
            P(("groups", "col"), None, None),
            P(("groups", "row"), None),
            P(("groups", "col"), None),
            P(("groups", "row")),
            P(("groups", "col")),
            P(("groups", "row"), "col", None),
            P(("groups", "row"), "col"),
        ),
        out_specs=(P(("groups", "row"), None), P(("groups", "col"), None)),
        check_vma=False,
    )
```

profile of v0, /device:TPU:6, one launch (start us, length us, event | category | flops | bytes accessed | tf_op | source)
XLA Modules:
  0.0 90.1 jit_solution(17878511693490725426)
XLA Ops:
  0.6 1.6 %copy-done = bf16[128,128,64]{1,2,0:T(8,128)(2,1)S(1)} copy-done((bf16[128,128,64]{1,2,0:T(8,128)(2,1)S(1)}, bf16[128,128,64]{1,2,0:T(8,128)(2,1)}, u32[]{:S(2)}) %copy-start) | copy-done | bytes 2097176
  2.2 1.0 %copy-done.1 = bf16[32,128,64]{1,2,0:T(8,128)(2,1)S(1)} copy-done((bf16[32,128,64]{1,2,0:T(8,128)(2,1)S(1)}, bf16[32,128,64]{1,2,0:T(8,128)(2,1)}, u32[]{:S(2)}) %copy-start.1) | copy-done | bytes 524312
  3.3 0.7 copy-done.4
  4.0 0.7 copy-done.5
  4.6 0.7 copy-done.6
  5.3 0.7 copy-done.7
  5.9 19.4 %scores_and_rows.1 = (f32[272,128,128]{2,1,0:T(8,128)S(1)}, f32[136,128]{1,0:T(8,128)S(1)}, s32[1024]{0:T(1024)S(1)}, f32[32,128]{1,0:T(8,128)S(1)}) custom-call(s32[32]{0:T(128)S(1)} %copy-done.5, s32[128]{0:T(128)S(1)} %copy-done.6, s32[8,32]{1,0:T(8,128)S(1)} %bitcast.8, s32[32]{0:T(128)S(1)} %bitcast.9, bf16[32,64,128]{2,1,0:T(8,128)(2,1)S(1)} %bitcast.7, ...), custom_call_target="tpu_custom_call" | custom-call | tf_op jit(solution)/shard_map/scores_and_rows/pallas_call | solution.py:296
  25.4 0.1 collective-permute-start.2
  25.4 0.8 collective-permute-start.1
  26.2 1.1 %collective-permute-start = (f32[32,128]{1,0:T(8,128)S(1)}, f32[32,128]{1,0:T(8,128)S(1)}, u32[]{:S(2)}, u32[]{:S(2)}) collective-permute-start(f32[32,128]{1,0:T(8,128)S(1)} %get-tuple-element.16.rest_0_.earlier_ref), channel_id=1, source_target_pairs={{0,1},{1,0},{2,3},{3,2},{4,5},{5,4},{6,7},{7,6},{8,9},{9,8},{10,11... | collective-permute-start | bytes 49160 | tf_op jit(solution)/shard_map/ppermute | solution.py:315
  27.3 1.3 %collective-permute-done.2.rest_3_ = f32[32,128]{1,0:T(8,128)S(1)} collective-permute-done((f32[32,128]{1,0:T(8,128)S(1)}, f32[32,128]{1,0:T(8,128)S(1)}, u32[]{:S(2)}, u32[]{:S(2)}) %collective-permute-start.2) | collective-permute-done | bytes 16416 | tf_op jit(solution)/shard_map/ppermute | solution.py:315
  28.6 0.7 collective-permute-done.1.rest_2_
  29.2 0.0 collective-permute-done.rest_1_
  29.2 9.6 %columns.2 = (f32[32,128]{1,0:T(8,128)S(1)}, f32[128,128]{1,0:T(8,128)S(1)}, f32[32,128,128]{2,1,0:T(8,128)S(1)}) custom-call(s32[1024]{0:T(1024)S(1)} %get-tuple-element.13.lists_ref, f32[272,128,128]{2,1,0:T(8,128)S(1)} %get-tuple-element.14.z_ref, f32[136,128]{1,0:T(8,128)S(1)} %get-tuple-element.15.touched_ref, f32[32,128]{1,0:T(8,128)S(1)} %copy-done.3, ...), custom_call_target="tpu_custom_call" | custom-call | tf_op jit(solution)/shard_map/columns/pallas_call | solution.py:296
  38.8 5.0 %collective-permute-start.5 = (f32[128,128]{1,0:T(8,128)S(1)}, f32[128,128]{1,0:T(8,128)S(1)}, u32[]{:S(2)}, u32[]{:S(2)}) collective-permute-start(f32[128,128]{1,0:T(8,128)S(1)} %get-tuple-element.19.rest_0_), channel_id=1, source_target_pairs={{0,12},{4,8},{8,4},{12,0},{1,13},{5,9},{9,5},{13,1},{2,14},{6,10},... | collective-permute-start | bytes 196616 | tf_op jit(solution)/shard_map/ppermute | solution.py:315
  43.8 0.0 collective-permute-start.4
  43.8 0.6 collective-permute-start.3
  44.5 2.1 %collective-permute-done.5.rest_3_ = f32[128,128]{1,0:T(8,128)S(1)} collective-permute-done((f32[128,128]{1,0:T(8,128)S(1)}, f32[128,128]{1,0:T(8,128)S(1)}, u32[]{:S(2)}, u32[]{:S(2)}) %collective-permute-start.5) | collective-permute-done | bytes 65568 | tf_op jit(solution)/shard_map/ppermute | solution.py:315
  46.6 2.6 %collective-permute-done.4.rest_2_ = f32[128,128]{1,0:T(8,128)S(1)} collective-permute-done((f32[128,128]{1,0:T(8,128)S(1)}, f32[128,128]{1,0:T(8,128)S(1)}, u32[]{:S(2)}, u32[]{:S(2)}) %collective-permute-start.4) | collective-permute-done | bytes 65568 | tf_op jit(solution)/shard_map/ppermute | solution.py:315
  49.2 0.0 collective-permute-done.3.rest_1_
  49.2 3.6 %rows.1 = (f32[136,128]{1,0:T(8,128)S(1)}, f32[32,128]{1,0:T(8,128)S(1)}) custom-call(s32[1024]{0:T(1024)S(1)} %get-tuple-element.13.lists_ref, f32[272,128,128]{2,1,0:T(8,128)S(1)} %get-tuple-element.14.z_ref, f32[32,128]{1,0:T(8,128)S(1)} %get-tuple-element.17.p_ref, f32[32,128,128]{2,1,0:T(8,128)S(1)} %get-tuple-element.18.pb_ref, ...), custom_call_target="tpu_custom_call" | custom-call | tf_op jit(solution)/shard_map/rows/pallas_call | solution.py:296
  52.8 0.7 collective-permute-start.8
  53.5 0.7 collective-permute-start.7
  54.2 0.5 collective-permute-start.6
  54.7 1.3 %collective-permute-done.8.rest_4_ = f32[32,128]{1,0:T(8,128)S(1)} collective-permute-done((f32[32,128]{1,0:T(8,128)S(1)}, f32[32,128]{1,0:T(8,128)S(1)}, u32[]{:S(2)}, u32[]{:S(2)}) %collective-permute-start.8) | collective-permute-done | bytes 16416 | tf_op jit(solution)/shard_map/ppermute | solution.py:315
  56.0 1.2 %collective-permute-done.7.rest_3_ = f32[32,128]{1,0:T(8,128)S(1)} collective-permute-done((f32[32,128]{1,0:T(8,128)S(1)}, f32[32,128]{1,0:T(8,128)S(1)}, u32[]{:S(2)}, u32[]{:S(2)}) %collective-permute-start.7) | collective-permute-done | bytes 16416 | tf_op jit(solution)/shard_map/ppermute | solution.py:315
  57.3 10.2 %columns.3 = (f32[32,128]{1,0:T(8,128)}, f32[128,128]{1,0:T(8,128)S(1)}) custom-call(s32[1024]{0:T(1024)S(1)} %get-tuple-element.13.lists_ref, f32[272,128,128]{2,1,0:T(8,128)S(1)} %get-tuple-element.14.z_ref, f32[136,128]{1,0:T(8,128)S(1)} %get-tuple-element.15.touched_ref, f32[32,128]{1,0:T(8,128)S(1)} %copy-done.3, ...), custom_call_target="tpu_custom_call" | custom-call | tf_op jit(solution)/shard_map/columns/pallas_call | solution.py:296
  67.4 16.9 %collective-permute-start.11 = (f32[128,128]{1,0:T(8,128)S(1)}, f32[128,128]{1,0:T(8,128)S(1)}, u32[]{:S(2)}, u32[]{:S(2)}) collective-permute-start(f32[128,128]{1,0:T(8,128)S(1)} %get-tuple-element.23.rest_0_), channel_id=1, source_target_pairs={{0,12},{4,8},{8,4},{12,0},{1,13},{5,9},{9,5},{13,1},{2,14},{6,10},... | collective-permute-start | bytes 196616 | tf_op jit(solution)/shard_map/ppermute | solution.py:315
  84.3 0.6 collective-permute-start.9
  84.9 1.7 %collective-permute-done.11.rest_3_ = f32[128,128]{1,0:T(8,128)S(1)} collective-permute-done((f32[128,128]{1,0:T(8,128)S(1)}, f32[128,128]{1,0:T(8,128)S(1)}, u32[]{:S(2)}, u32[]{:S(2)}) %collective-permute-start.11) | collective-permute-done | bytes 65568 | tf_op jit(solution)/shard_map/ppermute | solution.py:315
  86.6 2.8 %collective-permute-done.10.rest_2_ = f32[128,128]{1,0:T(8,128)S(1)} collective-permute-done((f32[128,128]{1,0:T(8,128)S(1)}, f32[128,128]{1,0:T(8,128)S(1)}, u32[]{:S(2)}, u32[]{:S(2)}) %collective-permute-start.10) | collective-permute-done | bytes 65568 | tf_op jit(solution)/shard_map/ppermute | solution.py:315
  89.5 0.7 target_field.1
  (13 shorter events, 0.0 us)
Async XLA Ops:
  0.6 1.6 %copy-start = (bf16[128,128,64]{1,2,0:T(8,128)(2,1)S(1)}, bf16[128,128,64]{1,2,0:T(8,128)(2,1)}, u32[]{:S(2)}) copy-start(bf16[128,128,64]{1,2,0:T(8,128)(2,1)} %param.9) | copy-start | bytes 6291460
  2.2 1.0 %copy-start.1 = (bf16[32,128,64]{1,2,0:T(8,128)(2,1)S(1)}, bf16[32,128,64]{1,2,0:T(8,128)(2,1)}, u32[]{:S(2)}) copy-start(bf16[32,128,64]{1,2,0:T(8,128)(2,1)} %param.8) | copy-start | bytes 1572868
  3.3 0.7 copy-start.4
  4.0 0.7 copy-start.5
  4.6 0.7 copy-start.6
  5.3 0.7 copy-start.7
  5.9 23.3 %copy-start.3 = (f32[32,128]{1,0:T(8,128)S(1)}, f32[32,128]{1,0:T(8,128)}, u32[]{:S(2)}) copy-start(f32[32,128]{1,0:T(8,128)} %logw_ref.6) | copy-start | bytes 49156
  25.4 3.2 %collective-permute-start.2 = (f32[32,128]{1,0:T(8,128)S(1)}, f32[32,128]{1,0:T(8,128)S(1)}, u32[]{:S(2)}, u32[]{:S(2)}) collective-permute-start(f32[32,128]{1,0:T(8,128)S(1)} %get-tuple-element.16.rest_0_.earlier_ref), channel_id=1, source_target_pairs={{0,3},{1,2},{2,1},{3,0},{4,7},{5,6},{6,5},{7,4},{8,11},{9,10},{10,... | collective-permute-start | bytes 49160 | tf_op jit(solution)/shard_map/ppermute | solution.py:315
  25.4 3.8 %collective-permute-start.1 = (f32[32,128]{1,0:T(8,128)S(1)}, f32[32,128]{1,0:T(8,128)S(1)}, u32[]{:S(2)}, u32[]{:S(2)}) collective-permute-start(f32[32,128]{1,0:T(8,128)S(1)} %get-tuple-element.16.rest_0_.earlier_ref), channel_id=1, source_target_pairs={{0,2},{1,3},{2,0},{3,1},{4,6},{5,7},{6,4},{7,5},{8,10},{9,11},{10,... | collective-permute-start | bytes 49160 | tf_op jit(solution)/shard_map/ppermute | solution.py:315
  26.2 3.0 %collective-permute-start = (f32[32,128]{1,0:T(8,128)S(1)}, f32[32,128]{1,0:T(8,128)S(1)}, u32[]{:S(2)}, u32[]{:S(2)}) collective-permute-start(f32[32,128]{1,0:T(8,128)S(1)} %get-tuple-element.16.rest_0_.earlier_ref), channel_id=1, source_target_pairs={{0,1},{1,0},{2,3},{3,2},{4,5},{5,4},{6,7},{7,6},{8,9},{9,8},{10,11... | collective-permute-start | bytes 49160 | tf_op jit(solution)/shard_map/ppermute | solution.py:315
  29.2 19.9 %copy-start.2 = (f32[128,128]{1,0:T(8,128)S(1)}, f32[128,128]{1,0:T(8,128)}, u32[]{:S(2)}) copy-start(f32[128,128]{1,0:T(8,128)} %logw_ref.7) | copy-start | bytes 196612
  38.8 7.8 %collective-permute-start.5 = (f32[128,128]{1,0:T(8,128)S(1)}, f32[128,128]{1,0:T(8,128)S(1)}, u32[]{:S(2)}, u32[]{:S(2)}) collective-permute-start(f32[128,128]{1,0:T(8,128)S(1)} %get-tuple-element.19.rest_0_), channel_id=1, source_target_pairs={{0,12},{4,8},{8,4},{12,0},{1,13},{5,9},{9,5},{13,1},{2,14},{6,10},... | collective-permute-start | bytes 196616 | tf_op jit(solution)/shard_map/ppermute | solution.py:315
  43.8 5.4 %collective-permute-start.4 = (f32[128,128]{1,0:T(8,128)S(1)}, f32[128,128]{1,0:T(8,128)S(1)}, u32[]{:S(2)}, u32[]{:S(2)}) collective-permute-start(f32[128,128]{1,0:T(8,128)S(1)} %get-tuple-element.19.rest_0_), channel_id=1, source_target_pairs={{0,8},{4,12},{8,0},{12,4},{1,9},{5,13},{9,1},{13,5},{2,10},{6,14},... | collective-permute-start | bytes 196616 | tf_op jit(solution)/shard_map/ppermute | solution.py:315
  43.8 5.4 %collective-permute-start.3 = (f32[128,128]{1,0:T(8,128)S(1)}, f32[128,128]{1,0:T(8,128)S(1)}, u32[]{:S(2)}, u32[]{:S(2)}) collective-permute-start(f32[128,128]{1,0:T(8,128)S(1)} %get-tuple-element.19.rest_0_), channel_id=1, source_target_pairs={{0,4},{4,0},{8,12},{12,8},{1,5},{5,1},{9,13},{13,9},{2,6},{6,2},{1... | collective-permute-start | bytes 196616 | tf_op jit(solution)/shard_map/ppermute | solution.py:315
  52.8 3.3 %collective-permute-start.8 = (f32[32,128]{1,0:T(8,128)S(1)}, f32[32,128]{1,0:T(8,128)S(1)}, u32[]{:S(2)}, u32[]{:S(2)}) collective-permute-start(f32[32,128]{1,0:T(8,128)S(1)} %get-tuple-element.21.rest_1_), channel_id=1, source_target_pairs={{0,3},{1,2},{2,1},{3,0},{4,7},{5,6},{6,5},{7,4},{8,11},{9,10},{10,... | collective-permute-start | bytes 49160 | tf_op jit(solution)/shard_map/ppermute | solution.py:315
  53.5 3.7 %collective-permute-start.7 = (f32[32,128]{1,0:T(8,128)S(1)}, f32[32,128]{1,0:T(8,128)S(1)}, u32[]{:S(2)}, u32[]{:S(2)}) collective-permute-start(f32[32,128]{1,0:T(8,128)S(1)} %get-tuple-element.21.rest_1_), channel_id=1, source_target_pairs={{0,2},{1,3},{2,0},{3,1},{4,6},{5,7},{6,4},{7,5},{8,10},{9,11},{10,... | collective-permute-start | bytes 49160 | tf_op jit(solution)/shard_map/ppermute | solution.py:315
  54.2 3.0 %collective-permute-start.6 = (f32[32,128]{1,0:T(8,128)S(1)}, f32[32,128]{1,0:T(8,128)S(1)}, u32[]{:S(2)}, u32[]{:S(2)}) collective-permute-start(f32[32,128]{1,0:T(8,128)S(1)} %get-tuple-element.21.rest_1_), channel_id=1, source_target_pairs={{0,1},{1,0},{2,3},{3,2},{4,5},{5,4},{6,7},{7,6},{8,9},{9,8},{10,11... | collective-permute-start | bytes 49160 | tf_op jit(solution)/shard_map/ppermute | solution.py:315
  67.4 19.2 %collective-permute-start.11 = (f32[128,128]{1,0:T(8,128)S(1)}, f32[128,128]{1,0:T(8,128)S(1)}, u32[]{:S(2)}, u32[]{:S(2)}) collective-permute-start(f32[128,128]{1,0:T(8,128)S(1)} %get-tuple-element.23.rest_0_), channel_id=1, source_target_pairs={{0,12},{4,8},{8,4},{12,0},{1,13},{5,9},{9,5},{13,1},{2,14},{6,10},... | collective-permute-start | bytes 196616 | tf_op jit(solution)/shard_map/ppermute | solution.py:315
  84.3 5.2 %collective-permute-start.10 = (f32[128,128]{1,0:T(8,128)S(1)}, f32[128,128]{1,0:T(8,128)S(1)}, u32[]{:S(2)}, u32[]{:S(2)}) collective-permute-start(f32[128,128]{1,0:T(8,128)S(1)} %get-tuple-element.23.rest_0_), channel_id=1, source_target_pairs={{0,8},{4,12},{8,0},{12,4},{1,9},{5,13},{9,1},{13,5},{2,10},{6,14},... | collective-permute-start | bytes 196616 | tf_op jit(solution)/shard_map/ppermute | solution.py:315
  84.3 5.2 %collective-permute-start.9 = (f32[128,128]{1,0:T(8,128)S(1)}, f32[128,128]{1,0:T(8,128)S(1)}, u32[]{:S(2)}, u32[]{:S(2)}) collective-permute-start(f32[128,128]{1,0:T(8,128)S(1)} %get-tuple-element.23.rest_0_), channel_id=1, source_target_pairs={{0,4},{4,0},{8,12},{12,8},{1,5},{5,1},{9,13},{13,9},{2,6},{6,2},{1... | collective-permute-start | bytes 196616 | tf_op jit(solution)/shard_map/ppermute | solution.py:315
where the time goes:
time: 90.1 us
  Pallas kernels  43.4 us (48%)
  starting transfers between devices  27 us (30%)
  waiting for transfers between devices  13.7 us (15%)
  local copies, waits for them, and re-layouts  5.28 us (6%)
    pallas_call x5, Pallas kernels, call(): pl.pallas_call(kernel, out_shape=outs, in_specs=[pl.BlockSpec(memory_spac...  43.4 us
    ppermute x12, starting transfers between devices, exchanged(): pieces.append(lax.ppermute(part, axis, pairs))  27 us
    ppermute x12, waiting for transfers between devices, exchanged(): pieces.append(lax.ppermute(part, axis, pairs))  13.7 us
    unnamed x16, local copies, waits for them, and re-layouts  5.28 us
  transfers between devices with their start and end apart: 12, of which 8 were waited for; matrix products, arithmetic and copies ran while one was open for 0% of the time, Pallas kernels for 0%

commit v1 on v0

--- a/solution.py
+++ b/solution.py
@@ -17,6 +17,7 @@
 ABSENT = -1e29
 SMALL = 2.0**-80
 CHUNK = 16
+LARGE_CHUNK = 64
 EXTRA = 16
 VMEM_LIMIT = 26 * 1024 * 1024
 
@@ -146,18 +147,19 @@
     return [high.astype(jnp.float32), middle.astype(jnp.float32), low.astype(jnp.float32)]
 
 
-def extra_rows(row, first, width):
-    place = lax.broadcasted_iota(jnp.int32, (EXTRA, width), 0)
-    result = jnp.where((place < 6) & ((place < first) | (place >= first + 3)), 1.0, 0.0)
+def extra_rows(row):
+    place = lax.broadcasted_iota(jnp.int32, (EXTRA, row.shape[1]), 0)
+    result = jnp.zeros(place.shape, jnp.float32)
     for k, term in enumerate(three_terms(row)):
-        result = jnp.where(place == first + k, term, result)
-    return result.astype(jnp.bfloat16)
+        result = jnp.where(place == k, term, result)
+    return result
 
 
 def first_kernel(
     ssz_any, tsz_any, pat_any, cnt_any, xt_any, yt_any,
     z_ref, touched_ref, lists_ref, out_ref,
-    ssz_ref, tsz_ref, pat_ref, cnt_ref, lists_smem, xt_ref, x_ref, y_ref, mask_ref, live_ref, acc_ref, sum_ref, sems,
+    ssz_ref, tsz_ref, pat_ref, cnt_ref, lists_smem, xt_ref, x_ref, y_ref, norm_ref, part_ref, live_ref, acc_ref, sum_ref,
+    sems,
 ):
     blocks, size = out_ref.shape
     dims = xt_ref.shape[1]
@@ -178,14 +180,26 @@
     copy_y.start()
     acc_ref[...] = jnp.zeros_like(acc_ref)
     touched_ref[...] = jnp.zeros_like(touched_ref)
+    lanes = lax.broadcasted_iota(jnp.int32, (1, size), 1)
+    ones = (lax.broadcasted_iota(jnp.int32, (EXTRA, size), 0) < 3).astype(jnp.bfloat16)
+
+    def pad_rows(t, carry):
+        y_ref[t, pl.ds(dims, EXTRA), :] = ones
+        return carry
+
+    lax.fori_loop(0, targets, pad_rows, 0, unroll=16)
     y_ref[targets] = jnp.zeros(y_ref.shape[1:], jnp.bfloat16)
-    mask_ref[pl.ds(targets, 8), :] = jnp.zeros((8, size), jnp.float32)
-    lanes = lax.broadcasted_iota(jnp.int32, (1, size), 1)
-    y_ref[targets, pl.ds(dims, EXTRA), :] = extra_rows(jnp.full((1, size), FLOOR, jnp.float32), 3, size)
+    norm_ref[pl.ds(targets, 8), :] = jnp.full((8, size), FLOOR, jnp.float32)
     for copy in small:
         copy.wait()
-
-    def list_block(s, p):
+    copy_x.wait()
+
+    def source(s, p):
+        xt = xt_ref[s].astype(jnp.float32)
+        live = lanes < ssz_ref[s]
+        norm = jnp.where(live, -0.5 * jnp.sum(xt * xt, axis=0, keepdims=True), FLOOR)
+        live_ref[pl.ds(s, 1), :] = live.astype(jnp.float32)
+        x_ref[s] = jnp.concatenate([xt, extra_rows(norm)], axis=0).T.astype(jnp.bfloat16)
         count = cnt_ref[s]
         for k in range(slots):
             lists_smem[p] = s
@@ -193,47 +207,47 @@
             p = p + (k < count).astype(jnp.int32)
         return p
 
-    pairs = lax.fori_loop(0, blocks, list_block, 0)
+    pairs = lax.fori_loop(0, blocks, source, 0, unroll=8)
     for k in range(CHUNK):
         lists_smem[pairs + k] = blocks - 1
         lists_smem[room + pairs + k] = targets
     lists_smem[room - 1] = pairs
     copy_lists = pltpu.make_async_copy(lists_smem, lists_ref, sems.at[6])
     copy_lists.start()
-    copy_x.wait()
-
-    def source(s, carry):
-        xt = xt_ref[s].astype(jnp.float32)
-        live = lanes < ssz_ref[s]
-        norm = jnp.where(live, -0.5 * jnp.sum(xt * xt, axis=0, keepdims=True), FLOOR)
-        live_ref[pl.ds(s, 1), :] = live.astype(jnp.float32)
-        extra = extra_rows(norm, 0, size).astype(jnp.float32)
-        x_ref[s] = jnp.concatenate([xt, extra], axis=0).T.astype(jnp.bfloat16)
-        return carry
-
-    lax.fori_loop(0, blocks, source, 0, unroll=4)
     copy_y.wait()
 
     def target(t, carry):
         yt = y_ref[t, pl.ds(0, dims), :].astype(jnp.float32)
-        live = lanes < tsz_ref[t]
-        norm = jnp.where(live, -0.5 * jnp.sum(yt * yt, axis=0, keepdims=True), FLOOR)
-        mask_ref[pl.ds(t, 1), :] = live.astype(jnp.float32)
-        y_ref[t, pl.ds(dims, EXTRA), :] = extra_rows(norm, 3, size)
-        return carry
-
-    lax.fori_loop(0, targets, target, 0, unroll=8)
-
-    def chunk(c, carry):
-        for k in range(CHUNK):
-            s, t = lists_smem[c * CHUNK + k], lists_smem[room + c * CHUNK + k]
-            z = jnp.dot(x_ref[s], y_ref[t], preferred_element_type=jnp.float32) * SCALE
-            z_ref[c * CHUNK + k] = z
+        part_ref[eight(t), :] = jnp.sum(folded(yt * yt), axis=0)
+        return carry
+
+    lax.fori_loop(0, targets, target, 0, unroll=16)
+    sizes = jnp.broadcast_to(tsz_ref[...].astype(jnp.float32), (size, targets)).T
+    mask = lax.broadcasted_iota(jnp.int32, (targets, size), 1).astype(jnp.float32) < sizes
+    norms = sum(every_eighth(part_ref, r, targets) for r in range(8))
+    norm_ref[pl.ds(0, targets), :] = jnp.where(mask, (-0.5 * SCALE) * norms, FLOOR)
+
+    def chunk(first, count):
+        for k in range(count):
+            s, t = lists_smem[first + k], lists_smem[room + first + k]
+            z = jnp.dot(x_ref[s], y_ref[t], preferred_element_type=jnp.float32) * SCALE + norm_ref[pl.ds(t, 1), :]
+            z_ref[first + k] = z
             acc_ref[s] += jnp.exp2(z)
-            touched_ref[pl.ds(t, 1), :] = mask_ref[pl.ds(t, 1), :]
-        return carry
-
-    lax.fori_loop(0, (pairs + CHUNK - 1) // CHUNK, chunk, 0)
+            touched_ref[pl.ds(t, 1), :] = jnp.ones((1, size), jnp.float32)
+
+    whole = pairs // LARGE_CHUNK
+
+    def large(c, carry):
+        chunk(c * LARGE_CHUNK, LARGE_CHUNK)
+        return carry
+
+    def rest(c, carry):
+        chunk(whole * LARGE_CHUNK + c * CHUNK, CHUNK)
+        return carry
+
+    lax.fori_loop(0, whole, large, 0)
+    lax.fori_loop(0, (pairs - whole * LARGE_CHUNK + CHUNK - 1) // CHUNK, rest, 0)
+    touched_ref[pl.ds(0, targets), :] = jnp.where(mask, touched_ref[pl.ds(0, targets), :], 0.0)
     collect(acc_ref, sum_ref)
     valid = live_ref[...] > 0.0
     row_result(sum_ref[...], 0.0, valid, z_ref, None, lists_smem, pairs, out_ref)
@@ -243,11 +257,18 @@
 def col_kernel(n_parts, has_q, last, lists_ref, z_ref, touched_ref, logw_ref, *rest):
     q_ref, rest = (rest[0], rest[1:]) if has_q else (None, rest)
     parts, rest = rest[:n_parts], rest[n_parts:]
-    p_ref, out_ref, pb_ref, lists_smem, acc_ref, top_ref, sem = rest
-    copy = pltpu.make_async_copy(lists_ref, lists_smem, sem)
+    if last:
+        field_any, out_ref, field_ref, p_ref, pb_ref, lists_smem, acc_ref, top_ref, sems = rest
+    else:
+        p_ref, out_ref, pb_ref, lists_smem, acc_ref, top_ref, sems = rest
+    copy = pltpu.make_async_copy(lists_ref, lists_smem, sems.at[0])
     copy.start()
     valid, total = merged([part[...] for part in parts])
     p_ref[...] = jnp.where(valid, LOG2E * logw_ref[...] - total, 0.0)
+    if last:
+        field_ref[...] = p_ref[...] * FIELD
+        copy_field = pltpu.make_async_copy(field_ref, field_any, sems.at[1])
+        copy_field.start()
     spread(p_ref, pb_ref)
     copy.wait()
     room = lists_smem.shape[0] // 2
@@ -255,7 +276,7 @@
         z_ref, pb_ref, q_ref, touched_ref, lists_smem, lists_smem[room - 1], acc_ref, top_ref, out_ref
     )
     if last:
-        p_ref[...] = p_ref[...] * FIELD
+        copy_field.wait()
 
 
 def row_kernel(n_parts, lists_ref, z_ref, p_ref, pb_ref, earlier_ref, logw_ref, *rest):
@@ -291,17 +312,21 @@
     out_ref[...] = jnp.where(valid, (LOG2E * logw_ref[...] - total) * FIELD, 0.0)
 
 
-def call(kernel, name, outs, scratch, args, spaces="v"):
+def call(kernel, name, outs, scratch, args, spaces="v", spaces_out="v"):
     where = {"v": pltpu.VMEM, "h": pltpu.HBM}
     return pl.pallas_call(
         kernel,
         out_shape=outs,
         in_specs=[pl.BlockSpec(memory_space=where[k]) for k in (spaces * len(args))[: len(args)]],
-        out_specs=[pl.BlockSpec(memory_space=pltpu.VMEM)] * len(outs),
+        out_specs=[pl.BlockSpec(memory_space=where[k]) for k in (spaces_out * len(outs))[: len(outs)]],
         scratch_shapes=scratch,
         name=name,
         compiler_params=pltpu.CompilerParams(vmem_limit_bytes=VMEM_LIMIT),
     )(*args)
+
+
+def in_hbm(array):
+    return pltpu.with_memory_space_constraint(array, pltpu.HBM)
 
 
 def exchanged(part, axis):
@@ -342,7 +367,7 @@
         ],
         [
             pltpu.SMEM((blocks,), i32),
-            pltpu.SMEM((targets,), i32),
+            pltpu.VMEM((1, targets), i32),
             pltpu.SMEM((slots, blocks), i32),
             pltpu.SMEM((blocks,), i32),
             lists_smem,
@@ -350,12 +375,13 @@
             pltpu.VMEM((blocks, size, dims + EXTRA), bf16),
             pltpu.VMEM((targets + 1, dims + EXTRA, size), bf16),
             pltpu.VMEM((targets + 8, size), f32),
+            pltpu.VMEM((targets * 8, size), f32),
             sums,
             wide,
             sums,
             dma((7,)),
         ],
-        [src_sizes, tgt_sizes, pattern[:, 0, :].T, counts[:, 0], xt, yt],
+        [in_hbm(array) for array in (src_sizes, tgt_sizes[None, :], pattern[:, 0, :].T, counts[:, 0], xt, yt)],
         "h",
     )
     first_part = row_part
@@ -368,8 +394,9 @@
             "columns",
             [struct((blocks, size), f32), struct((targets, size), f32)]
             + ([] if last else [struct((blocks, size, size), f32)]),
-            ([wide] if last else []) + [lists_smem, acc_col, acc_col, dma],
+            ([sums, sums, wide] if last else []) + [lists_smem, acc_col, acc_col, dma((2,))],
             [lists, z, touched, src_logw] + ([] if q is None else [q]) + row_parts,
+            spaces_out="hv" if last else "vvv",
         )
         p, col_part, *pb = results
         col_parts = exchanged(col_part, "row")

time: 90.1 us -> 82.5 us (0.916)
  local copies, waits for them, and re-layouts: 5.28 us -> 0.01 us
  waiting for transfers between devices: 13.7 us -> 10.3 us
  Pallas kernels: 43.4 us -> 45.9 us
  starting transfers between devices: 27 us -> 24.8 us
    unnamed x16 -> x4, local copies, waits for them, and re-layouts: 5.28 us -> 0.01 us
    ppermute x12, waiting for transfers between devices: 13.7 us -> 10.3 us  [exchanged(): pieces.append(lax.ppermute(part, axis, pairs))]
    pallas_call x5, Pallas kernels: 43.4 us -> 45.9 us  [call(): pl.pallas_call(kernel, out_shape=outs, in_specs=[pl.BlockSpec(memory_spac...]
    ppermute x12, starting transfers between devices: 27 us -> 24.8 us  [exchanged(): pieces.append(lax.ppermute(part, axis, pairs))]
where the time goes in v1:
time: 82.5 us; the launch traced here: 81.7 us
  Pallas kernels  45.9 us (56%)
  starting transfers between devices  24.8 us (30%)
  waiting for transfers between devices  10.3 us (12%)
    pallas_call x5, Pallas kernels, call(): pl.pallas_call(kernel, out_shape=outs, in_specs=[pl.BlockSpec(memory_spac...  45.9 us
    ppermute x12, starting transfers between devices, exchanged(): pieces.append(lax.ppermute(part, axis, pairs))  24.8 us
    ppermute x12, waiting for transfers between devices, exchanged(): pieces.append(lax.ppermute(part, axis, pairs))  10.3 us
  transfers between devices with their start and end apart: 12, of which 8 were waited for; matrix products, arithmetic and copies ran while one was open for 0% of the time, Pallas kernels for 0%

profile of v1, /device:TPU:6, one launch (start us, length us, event | category | flops | bytes accessed | tf_op | source)
XLA Modules:
  0.0 81.7 jit_solution(1492346096986327273)
XLA Ops:
  0.6 0.0 copy-start.1
  0.6 19.7 %scores_and_rows.1 = (f32[272,128,128]{2,1,0:T(8,128)S(1)}, f32[136,128]{1,0:T(8,128)S(1)}, s32[1024]{0:T(1024)S(1)}, f32[32,128]{1,0:T(8,128)S(1)}) custom-call(s32[32]{0:T(128)} %ssz_any.1, s32[1,128]{1,0:T(1,128)} %bitcast.10, s32[8,32]{1,0:T(8,128)} %bitcast.9, s32[32]{0:T(128)} %bitcast.11, bf16[32,64,128]{2,1,0:T(8,128)(2,1)} %bitcast.8, ...), custom_call_target="tpu_custom_call" | custom-call | tf_op jit(solution)/shard_map/scores_and_rows/pallas_call | solution.py:317
  20.3 0.1 collective-permute-start.2
  20.4 0.5 collective-permute-start.1
  21.0 1.3 %collective-permute-start = (f32[32,128]{1,0:T(8,128)S(1)}, f32[32,128]{1,0:T(8,128)S(1)}, u32[]{:S(2)}, u32[]{:S(2)}) collective-permute-start(f32[32,128]{1,0:T(8,128)S(1)} %get-tuple-element.16.rest_0_.earlier_ref), channel_id=1, source_target_pairs={{0,1},{1,0},{2,3},{3,2},{4,5},{5,4},{6,7},{7,6},{8,9},{9,8},{10,11... | collective-permute-start | bytes 49160 | tf_op jit(solution)/shard_map/ppermute | solution.py:340
  22.3 1.3 %collective-permute-done.2.rest_3_ = f32[32,128]{1,0:T(8,128)S(1)} collective-permute-done((f32[32,128]{1,0:T(8,128)S(1)}, f32[32,128]{1,0:T(8,128)S(1)}, u32[]{:S(2)}, u32[]{:S(2)}) %collective-permute-start.2) | collective-permute-done | bytes 16416 | tf_op jit(solution)/shard_map/ppermute | solution.py:340
  23.6 0.7 collective-permute-done.1.rest_2_
  24.2 0.0 collective-permute-done.rest_1_
  24.2 0.0 copy-done.1
  24.2 10.8 %columns.2 = (f32[32,128]{1,0:T(8,128)S(1)}, f32[128,128]{1,0:T(8,128)S(1)}, f32[32,128,128]{2,1,0:T(8,128)S(1)}) custom-call(s32[1024]{0:T(1024)S(1)} %get-tuple-element.13.lists_ref, f32[272,128,128]{2,1,0:T(8,128)S(1)} %get-tuple-element.14.z_ref, f32[136,128]{1,0:T(8,128)S(1)} %get-tuple-element.15.touched_ref, f32[32,128]{1,0:T(8,128)S(1)} %copy-done.1, ...), custom_call_target="tpu_custom_call" | custom-call | tf_op jit(solution)/shard_map/columns/pallas_call | solution.py:317
  35.1 0.8 collective-permute-start.5
  35.9 1.7 %collective-permute-start.4 = (f32[128,128]{1,0:T(8,128)S(1)}, f32[128,128]{1,0:T(8,128)S(1)}, u32[]{:S(2)}, u32[]{:S(2)}) collective-permute-start(f32[128,128]{1,0:T(8,128)S(1)} %get-tuple-element.19.rest_0_), channel_id=1, source_target_pairs={{0,8},{4,12},{8,0},{12,4},{1,9},{5,13},{9,1},{13,5},{2,10},{6,14},... | collective-permute-start | bytes 196616 | tf_op jit(solution)/shard_map/ppermute | solution.py:340
  37.6 1.9 %collective-permute-start.3 = (f32[128,128]{1,0:T(8,128)S(1)}, f32[128,128]{1,0:T(8,128)S(1)}, u32[]{:S(2)}, u32[]{:S(2)}) collective-permute-start(f32[128,128]{1,0:T(8,128)S(1)} %get-tuple-element.19.rest_0_), channel_id=1, source_target_pairs={{0,4},{4,0},{8,12},{12,8},{1,5},{5,1},{9,13},{13,9},{2,6},{6,2},{1... | collective-permute-start | bytes 196616 | tf_op jit(solution)/shard_map/ppermute | solution.py:340
  39.5 1.8 %collective-permute-done.5.rest_3_ = f32[128,128]{1,0:T(8,128)S(1)} collective-permute-done((f32[128,128]{1,0:T(8,128)S(1)}, f32[128,128]{1,0:T(8,128)S(1)}, u32[]{:S(2)}, u32[]{:S(2)}) %collective-permute-start.5) | collective-permute-done | bytes 65568 | tf_op jit(solution)/shard_map/ppermute | solution.py:340
  41.3 1.4 %collective-permute-done.4.rest_2_ = f32[128,128]{1,0:T(8,128)S(1)} collective-permute-done((f32[128,128]{1,0:T(8,128)S(1)}, f32[128,128]{1,0:T(8,128)S(1)}, u32[]{:S(2)}, u32[]{:S(2)}) %collective-permute-start.4) | collective-permute-done | bytes 65568 | tf_op jit(solution)/shard_map/ppermute | solution.py:340
  42.7 0.0 collective-permute-done.3.rest_1_
  42.7 0.0 copy-done
  42.7 3.8 %rows.1 = (f32[136,128]{1,0:T(8,128)S(1)}, f32[32,128]{1,0:T(8,128)S(1)}) custom-call(s32[1024]{0:T(1024)S(1)} %get-tuple-element.13.lists_ref, f32[272,128,128]{2,1,0:T(8,128)S(1)} %get-tuple-element.14.z_ref, f32[32,128]{1,0:T(8,128)S(1)} %get-tuple-element.17.p_ref, f32[32,128,128]{2,1,0:T(8,128)S(1)} %get-tuple-element.18.pb_ref, ...), custom_call_target="tpu_custom_call" | custom-call | tf_op jit(solution)/shard_map/rows/pallas_call | solution.py:317
  46.5 0.7 collective-permute-start.8
  47.3 13.2 %collective-permute-start.7 = (f32[32,128]{1,0:T(8,128)S(1)}, f32[32,128]{1,0:T(8,128)S(1)}, u32[]{:S(2)}, u32[]{:S(2)}) collective-permute-start(f32[32,128]{1,0:T(8,128)S(1)} %get-tuple-element.21.rest_1_), channel_id=1, source_target_pairs={{0,2},{1,3},{2,0},{3,1},{4,6},{5,7},{6,4},{7,5},{8,10},{9,11},{10,... | collective-permute-start | bytes 49160 | tf_op jit(solution)/shard_map/ppermute | solution.py:340
  60.5 0.0 collective-permute-start.6
  60.5 0.0 collective-permute-done.8.rest_4_
  60.5 1.8 %collective-permute-done.7.rest_3_ = f32[32,128]{1,0:T(8,128)S(1)} collective-permute-done((f32[32,128]{1,0:T(8,128)S(1)}, f32[32,128]{1,0:T(8,128)S(1)}, u32[]{:S(2)}, u32[]{:S(2)}) %collective-permute-start.7) | collective-permute-done | bytes 16416 | tf_op jit(solution)/shard_map/ppermute | solution.py:340
  62.3 0.0 collective-permute-done.6.rest_2_
  62.3 10.9 %columns.3 = (f32[32,128]{1,0:T(8,128)}, f32[128,128]{1,0:T(8,128)S(1)}) custom-call(s32[1024]{0:T(1024)S(1)} %get-tuple-element.13.lists_ref, f32[272,128,128]{2,1,0:T(8,128)S(1)} %get-tuple-element.14.z_ref, f32[136,128]{1,0:T(8,128)S(1)} %get-tuple-element.15.touched_ref, f32[32,128]{1,0:T(8,128)S(1)} %copy-done.1, ...), custom_call_target="tpu_custom_call" | custom-call | tf_op jit(solution)/shard_map/columns/pallas_call | solution.py:317
  73.2 0.1 collective-permute-start.11
  73.3 0.5 collective-permute-start.10
  73.7 3.9 %collective-permute-start.9 = (f32[128,128]{1,0:T(8,128)S(1)}, f32[128,128]{1,0:T(8,128)S(1)}, u32[]{:S(2)}, u32[]{:S(2)}) collective-permute-start(f32[128,128]{1,0:T(8,128)S(1)} %get-tuple-element.23.rest_0_), channel_id=1, source_target_pairs={{0,4},{4,0},{8,12},{12,8},{1,5},{5,1},{9,13},{13,9},{2,6},{6,2},{1... | collective-permute-start | bytes 196616 | tf_op jit(solution)/shard_map/ppermute | solution.py:340
  77.7 2.5 %collective-permute-done.11.rest_3_ = f32[128,128]{1,0:T(8,128)S(1)} collective-permute-done((f32[128,128]{1,0:T(8,128)S(1)}, f32[128,128]{1,0:T(8,128)S(1)}, u32[]{:S(2)}, u32[]{:S(2)}) %collective-permute-start.11) | collective-permute-done | bytes 65568 | tf_op jit(solution)/shard_map/ppermute | solution.py:340
  80.1 0.4 collective-permute-done.10.rest_2_
  80.5 0.5 collective-permute-done.9.rest_1_
  81.0 0.7 target_field.1
  (1 shorter events, 0.0 us)
Async XLA Ops:
  0.6 23.6 %copy-start.1 = (f32[32,128]{1,0:T(8,128)S(1)}, f32[32,128]{1,0:T(8,128)}, u32[]{:S(2)}) copy-start(f32[32,128]{1,0:T(8,128)} %logw_ref.6) | copy-start | bytes 49156
  20.3 3.2 %collective-permute-start.2 = (f32[32,128]{1,0:T(8,128)S(1)}, f32[32,128]{1,0:T(8,128)S(1)}, u32[]{:S(2)}, u32[]{:S(2)}) collective-permute-start(f32[32,128]{1,0:T(8,128)S(1)} %get-tuple-element.16.rest_0_.earlier_ref), channel_id=1, source_target_pairs={{0,3},{1,2},{2,1},{3,0},{4,7},{5,6},{6,5},{7,4},{8,11},{9,10},{10,... | collective-permute-start | bytes 49160 | tf_op jit(solution)/shard_map/ppermute | solution.py:340
  20.4 3.8 %collective-permute-start.1 = (f32[32,128]{1,0:T(8,128)S(1)}, f32[32,128]{1,0:T(8,128)S(1)}, u32[]{:S(2)}, u32[]{:S(2)}) collective-permute-start(f32[32,128]{1,0:T(8,128)S(1)} %get-tuple-element.16.rest_0_.earlier_ref), channel_id=1, source_target_pairs={{0,2},{1,3},{2,0},{3,1},{4,6},{5,7},{6,4},{7,5},{8,10},{9,11},{10,... | collective-permute-start | bytes 49160 | tf_op jit(solution)/shard_map/ppermute | solution.py:340
  21.0 3.3 %collective-permute-start = (f32[32,128]{1,0:T(8,128)S(1)}, f32[32,128]{1,0:T(8,128)S(1)}, u32[]{:S(2)}, u32[]{:S(2)}) collective-permute-start(f32[32,128]{1,0:T(8,128)S(1)} %get-tuple-element.16.rest_0_.earlier_ref), channel_id=1, source_target_pairs={{0,1},{1,0},{2,3},{3,2},{4,5},{5,4},{6,7},{7,6},{8,9},{9,8},{10,11... | collective-permute-start | bytes 49160 | tf_op jit(solution)/shard_map/ppermute | solution.py:340
  24.2 18.5 %copy-start = (f32[128,128]{1,0:T(8,128)S(1)}, f32[128,128]{1,0:T(8,128)}, u32[]{:S(2)}) copy-start(f32[128,128]{1,0:T(8,128)} %logw_ref.7) | copy-start | bytes 196612
  35.1 6.2 %collective-permute-start.5 = (f32[128,128]{1,0:T(8,128)S(1)}, f32[128,128]{1,0:T(8,128)S(1)}, u32[]{:S(2)}, u32[]{:S(2)}) collective-permute-start(f32[128,128]{1,0:T(8,128)S(1)} %get-tuple-element.19.rest_0_), channel_id=1, source_target_pairs={{0,12},{4,8},{8,4},{12,0},{1,13},{5,9},{9,5},{13,1},{2,14},{6,10},... | collective-permute-start | bytes 196616 | tf_op jit(solution)/shard_map/ppermute | solution.py:340
  35.9 6.9 %collective-permute-start.4 = (f32[128,128]{1,0:T(8,128)S(1)}, f32[128,128]{1,0:T(8,128)S(1)}, u32[]{:S(2)}, u32[]{:S(2)}) collective-permute-start(f32[128,128]{1,0:T(8,128)S(1)} %get-tuple-element.19.rest_0_), channel_id=1, source_target_pairs={{0,8},{4,12},{8,0},{12,4},{1,9},{5,13},{9,1},{13,5},{2,10},{6,14},... | collective-permute-start | bytes 196616 | tf_op jit(solution)/shard_map/ppermute | solution.py:340
  37.6 5.1 %collective-permute-start.3 = (f32[128,128]{1,0:T(8,128)S(1)}, f32[128,128]{1,0:T(8,128)S(1)}, u32[]{:S(2)}, u32[]{:S(2)}) collective-permute-start(f32[128,128]{1,0:T(8,128)S(1)} %get-tuple-element.19.rest_0_), channel_id=1, source_target_pairs={{0,4},{4,0},{8,12},{12,8},{1,5},{5,1},{9,13},{13,9},{2,6},{6,2},{1... | collective-permute-start | bytes 196616 | tf_op jit(solution)/shard_map/ppermute | solution.py:340
  46.5 14.0 %collective-permute-start.8 = (f32[32,128]{1,0:T(8,128)S(1)}, f32[32,128]{1,0:T(8,128)S(1)}, u32[]{:S(2)}, u32[]{:S(2)}) collective-permute-start(f32[32,128]{1,0:T(8,128)S(1)} %get-tuple-element.21.rest_1_), channel_id=1, source_target_pairs={{0,3},{1,2},{2,1},{3,0},{4,7},{5,6},{6,5},{7,4},{8,11},{9,10},{10,... | collective-permute-start | bytes 49160 | tf_op jit(solution)/shard_map/ppermute | solution.py:340
  47.3 15.0 %collective-permute-start.7 = (f32[32,128]{1,0:T(8,128)S(1)}, f32[32,128]{1,0:T(8,128)S(1)}, u32[]{:S(2)}, u32[]{:S(2)}) collective-permute-start(f32[32,128]{1,0:T(8,128)S(1)} %get-tuple-element.21.rest_1_), channel_id=1, source_target_pairs={{0,2},{1,3},{2,0},{3,1},{4,6},{5,7},{6,4},{7,5},{8,10},{9,11},{10,... | collective-permute-start | bytes 49160 | tf_op jit(solution)/shard_map/ppermute | solution.py:340
  60.5 1.8 %collective-permute-start.6 = (f32[32,128]{1,0:T(8,128)S(1)}, f32[32,128]{1,0:T(8,128)S(1)}, u32[]{:S(2)}, u32[]{:S(2)}) collective-permute-start(f32[32,128]{1,0:T(8,128)S(1)} %get-tuple-element.21.rest_1_), channel_id=1, source_target_pairs={{0,1},{1,0},{2,3},{3,2},{4,5},{5,4},{6,7},{7,6},{8,9},{9,8},{10,11... | collective-permute-start | bytes 49160 | tf_op jit(solution)/shard_map/ppermute | solution.py:340
  73.2 6.9 %collective-permute-start.11 = (f32[128,128]{1,0:T(8,128)S(1)}, f32[128,128]{1,0:T(8,128)S(1)}, u32[]{:S(2)}, u32[]{:S(2)}) collective-permute-start(f32[128,128]{1,0:T(8,128)S(1)} %get-tuple-element.23.rest_0_), channel_id=1, source_target_pairs={{0,12},{4,8},{8,4},{12,0},{1,13},{5,9},{9,5},{13,1},{2,14},{6,10},... | collective-permute-start | bytes 196616 | tf_op jit(solution)/shard_map/ppermute | solution.py:340
  73.3 7.2 %collective-permute-start.10 = (f32[128,128]{1,0:T(8,128)S(1)}, f32[128,128]{1,0:T(8,128)S(1)}, u32[]{:S(2)}, u32[]{:S(2)}) collective-permute-start(f32[128,128]{1,0:T(8,128)S(1)} %get-tuple-element.23.rest_0_), channel_id=1, source_target_pairs={{0,8},{4,12},{8,0},{12,4},{1,9},{5,13},{9,1},{13,5},{2,10},{6,14},... | collective-permute-start | bytes 196616 | tf_op jit(solution)/shard_map/ppermute | solution.py:340
  73.7 7.2 %collective-permute-start.9 = (f32[128,128]{1,0:T(8,128)S(1)}, f32[128,128]{1,0:T(8,128)S(1)}, u32[]{:S(2)}, u32[]{:S(2)}) collective-permute-start(f32[128,128]{1,0:T(8,128)S(1)} %get-tuple-element.23.rest_0_), channel_id=1, source_target_pairs={{0,4},{4,0},{8,12},{12,8},{1,5},{5,1},{9,13},{13,9},{2,6},{6,2},{1... | collective-permute-start | bytes 196616 | tf_op jit(solution)/shard_map/ppermute | solution.py:340
